TPU v7x, 256 devices: a whole 4x4x8 slice. The times are simulated.
256 devices in a mesh: ctx: 64 (over z, x, core), head: 4 (over y).
Axes of the slice: x: 4, y: 4, z: 8, core: 2. Of those that a mesh axis runs over, the one named last changes fastest.
Arguments:
- query_raw: bfloat16 [65536, 4096], P('ctx', 'head'), may hold values from -6 to 6
- key_raw: bfloat16 [65536, 4096], P('ctx', 'head'), may hold values from -6 to 6
- value_raw: bfloat16 [65536, 4096], P('ctx', 'head'), may hold values from -6 to 6
- gate_raw: bfloat16 [65536, 4096], P('ctx', 'head'), may hold values from -6 to 6
- conv_weight: float32 [3, 4, 4096], P(None, None, 'head'), as said below
- norm_gain: float32 [4096], P('head'), may hold values from 0.1 to 1.9
Outputs:
- attended: bfloat16 [65536, 4096], P('ctx', 'head')
Inputs may be any that keep to these rules, and one draw needn't show every extreme that they name: `conv_weight`: taps of the short convolutions.
All inputs are finite; a program needn't handle non-finite values.
Results may differ from a plain program's by a relative error of at most 0.0061.
Values may be sent and summed in bfloat16 or wider, within the bound.
A program may use at most 128 MiB of HBM per device.

v0:
```python
import jax
import jax.numpy as jnp
from jax import lax
from jax.sharding import PartitionSpec as P

DH = 128
KW = 4
BLOCK = 512


def from_behind(array, axis, by):
    count = lax.axis_size(axis)
    pairs = [(i, i + by) for i in range(count) if 0 <= i + by < count]
    return lax.ppermute(array, axis, pairs)


def swapped(value, axis, stride):
    mask = 2**stride
    pairs = [(source, source ^ mask) for source in range(lax.axis_size(axis))]
    return lax.ppermute(value, axis, pairs)


def convolve(raw_rows, tail_rows, tap_weights, tok_rows):
    extended = jnp.concatenate([tail_rows, raw_rows], axis=0).astype(jnp.float32)
    result = tap_weights[0][None, :] * extended[0:tok_rows]
    for offset in range(1, KW):
        result = result + tap_weights[offset][None, :] * extended[offset : offset + tok_rows]
    return result


def body(query_raw, key_raw, value_raw, gate_raw, conv_weight, norm_gain):
    tok_rows, channels = query_raw.shape
    head_count = channels // DH
    rim_rows = KW - 1
    tails = from_behind(
        (
            query_raw[tok_rows - rim_rows :],
            key_raw[tok_rows - rim_rows :],
            value_raw[tok_rows - rim_rows :],
        ),
        "ctx",
        1,
    )
    queries = (
        jax.nn.silu(convolve(query_raw, tails[0], conv_weight[0], tok_rows)) * DH ** (-0.5)
    ).astype(jnp.bfloat16)
    keys_bf = jax.nn.silu(convolve(key_raw, tails[1], conv_weight[1], tok_rows)).astype(
        jnp.bfloat16
    )
    values_bf = convolve(value_raw, tails[2], conv_weight[2], tok_rows).astype(jnp.bfloat16)
    block_count = tok_rows // BLOCK
    query_blk = queries.reshape(block_count, BLOCK, head_count, DH)
    key_blk = keys_bf.reshape(block_count, BLOCK, head_count, DH)
    value_blk = values_bf.reshape(block_count, BLOCK, head_count, DH)
    causal = (jnp.arange(BLOCK)[:, None] >= jnp.arange(BLOCK)[None, :])[None, None]
    scores = jnp.einsum("nqhd,nkhd->nhqk", query_blk, key_blk, preferred_element_type=jnp.float32)
    weights = jnp.where(causal, scores, 0.0).astype(jnp.bfloat16)
    inner = jnp.einsum("nhqk,nkhd->nqhd", weights, value_blk, preferred_element_type=jnp.float32)
    block_states = jnp.einsum(
        "nkhd,nkhe->nhde", key_blk, value_blk, preferred_element_type=jnp.float32
    )
    local_total = jnp.sum(block_states, axis=0)
    empty = jnp.zeros_like(local_total)
    running = jnp.cumsum(block_states, axis=0)
    earlier_blocks = jnp.concatenate([empty[None], running[:-1]], axis=0)
    group_size = min(16, lax.axis_size("ctx"))
    device_index = lax.axis_index("ctx")
    group_total = local_total
    within = empty
    for bit_pos in range(group_size.bit_length() - 1):
        partner = swapped(group_total, "ctx", bit_pos)
        upper = device_index // 2**bit_pos % 2 == 1
        within = within + jnp.where(upper, partner, 0.0)
        group_total = group_total + partner
    carried = empty
    for section in range(lax.axis_size("ctx") // group_size - 1):
        carried = from_behind(carried + group_total, "ctx", group_size)
    incoming = carried + within
    states = (incoming[None] + earlier_blocks).astype(jnp.bfloat16)
    outer = jnp.einsum("nqhd,nhde->nqhe", query_blk, states, preferred_element_type=jnp.float32)
    mixed = (inner + outer).reshape(tok_rows, channels)
    square = lax.psum(jnp.sum(mixed * mixed, axis=1), "head")
    total_channels = channels * lax.axis_size("head")
    factor = lax.rsqrt(square / total_channels + 1e-06)
    output = (
        mixed * factor[:, None] * norm_gain[None, :] * jax.nn.sigmoid(gate_raw.astype(jnp.float32))
    )
    return output.astype(jnp.bfloat16)


def solution(mesh):
    placed = (
        P("ctx", "head"),
        P("ctx", "head"),
        P("ctx", "head"),
        P("ctx", "head"),
        P(None, None, "head"),
        P("head"),
    )
    return jax.shard_map(
        body, mesh=mesh, in_specs=placed, out_specs=P("ctx", "head"), check_vma=False
    )
```

profile of v0, /device:TPU:96, one launch (start us, length us, event | category | flops | bytes accessed | tf_op | source)
XLA Modules:
  0.0 179.5 jit_solution(12985579713640560821)
XLA Ops:
  3.4 3.5 %collective-permute-start = (bf16[3,1024]{1,0:T(4,128)(2,1)S(1)}, bf16[3,1024]{1,0:T(4,128)(2,1)S(1)}, u32[]{:S(2)}, u32[]{:S(2)}) collective-permute-start(bf16[3,1024]{1,0:T(4,128)(2,1)S(1)} %slice.112), channel_id=1, source_target_pairs={{0,4},{4,8},{8,12},{12,16},{16,20},{20,24},{24,28},{28,32},{32,36}... | collective-permute-start | bytes 18440 | tf_op jit(solution)/shard_map/ppermute | solution.py:14
  7.9 2.2 %maximum_convert_fusion.2 = f32[1027,1024]{1,0:T(8,128)S(1)} fusion(bf16[1024,1024]{1,0:T(8,128)(2,1)} %param.7, bf16[3,1024]{1,0:T(4,128)(2,1)S(1)} %collective-permute-done.2), kind=kLoop, calls=%fused_computation.37 | loop fusion | flops 4206592 | bytes 6309888 | tf_op jit(solution)/shard_map/convert_element_type | solution.py:24
  10.1 2.6 %fusion.19 = bf16[128,8,8,128]{3,1,2,0:T(8,128)(2,1)S(1)} fusion(f32[1027,1024]{1,0:T(8,128)S(1)} %maximum_convert_fusion.2, f32[1024]{0:T(1024)S(1)} %bitcast.59, f32[1024]{0:T(1024)S(1)} %bitcast.60, f32[1024]{0:T(1024)S(1)} %bitcast.57, f32[1024]{0:T(1024)S(1)} %bitcast.58), kind=kLoop, calls=%fused_computation.39 | loop fusion | flops 12582912 | bytes 18890752
  13.4 2.6 %copy.13 = bf16[2,512,8,128]{1,3,2,0:T(8,128)(2,1)} copy(bf16[2,512,8,128]{3,2,1,0:T(8,128)(2,1)S(1)} %bitcast.42) | data formatting | bytes 4194304 | tf_op jit(solution)/shard_map/reshape | solution.py:53
  15.9 2.2 %maximum_convert_fusion = f32[1027,1024]{1,0:T(8,128)S(1)} fusion(bf16[1024,1024]{1,0:T(8,128)(2,1)} %param.8, bf16[3,1024]{1,0:T(4,128)(2,1)S(1)} %collective-permute-done), kind=kLoop, calls=%fused_computation.35 | loop fusion | flops 4206592 | bytes 6309888 | tf_op jit(solution)/shard_map/convert_element_type | solution.py:24
  18.1 1.9 %fusion.18 = bf16[128,8,8,128]{3,1,2,0:T(8,128)(2,1)S(1)} fusion(f32[1027,1024]{1,0:T(8,128)S(1)} %maximum_convert_fusion, f32[1024]{0:T(1024)S(1)} %bitcast.54, f32[1024]{0:T(1024)S(1)} %bitcast.55, f32[1024]{0:T(1024)S(1)} %bitcast.56, f32[1024]{0:T(1024)S(1)} %bitcast.53), kind=kLoop, calls=%fused_computation.38 | loop fusion | flops 8388608 | bytes 18890752
  27.1 12.5 %collective-permute-done.4 = f32[8,128,128]{2,1,0:T(8,128)S(1)} collective-permute-done((f32[8,128,128]{2,1,0:T(8,128)S(1)}, f32[8,128,128]{2,1,0:T(8,128)S(1)}, u32[]{:S(2)}, u32[]{:S(2)}) %collective-permute-start.4) | collective-permute-done | bytes 524320 | tf_op jit(solution)/shard_map/ppermute | solution.py:20
  39.6 4.1 %collective-permute-start.5 = (f32[8,128,128]{2,1,0:T(8,128)S(1)}, f32[8,128,128]{2,1,0:T(8,128)S(1)}, u32[]{:S(2)}, u32[]{:S(2)}) collective-permute-start(f32[8,128,128]{2,1,0:T(8,128)S(1)} %add.120), channel_id=1, source_target_pairs={{0,16},{4,20},{8,24},{12,28},{16,0},{20,4},{24,8},{28,12},{32,48},... | collective-permute-start | bytes 1572872 | tf_op jit(solution)/shard_map/ppermute | solution.py:20
  43.7 11.7 %collective-permute-done.5 = f32[8,128,128]{2,1,0:T(8,128)S(1)} collective-permute-done((f32[8,128,128]{2,1,0:T(8,128)S(1)}, f32[8,128,128]{2,1,0:T(8,128)S(1)}, u32[]{:S(2)}, u32[]{:S(2)}) %collective-permute-start.5) | collective-permute-done | bytes 524320 | tf_op jit(solution)/shard_map/ppermute | solution.py:20
  58.3 10.2 %collective-permute-done.6 = f32[8,128,128]{2,1,0:T(8,128)S(1)} collective-permute-done((f32[8,128,128]{2,1,0:T(8,128)S(1)}, f32[8,128,128]{2,1,0:T(8,128)S(1)}, u32[]{:S(2)}, u32[]{:S(2)}) %collective-permute-start.6) | collective-permute-done | bytes 524320 | tf_op jit(solution)/shard_map/ppermute | solution.py:20
  68.5 4.1 %collective-permute-start.7 = (f32[8,128,128]{2,1,0:T(8,128)S(1)}, f32[8,128,128]{2,1,0:T(8,128)}, u32[]{:S(2)}, u32[]{:S(2)}) collective-permute-start(f32[8,128,128]{2,1,0:T(8,128)S(1)} %add.122), channel_id=1, source_target_pairs={{0,64},{4,68},{8,72},{12,76},{16,80},{20,84},{24,88},{28,92},{32,9... | collective-permute-start | bytes 1572872 | tf_op jit(solution)/shard_map/ppermute | solution.py:14
  72.9 2.2 %maximum_convert_fusion.1 = f32[1027,1024]{1,0:T(8,128)S(1)} fusion(bf16[1024,1024]{1,0:T(8,128)(2,1)} %param.6, bf16[3,1024]{1,0:T(4,128)(2,1)S(1)} %collective-permute-done.1), kind=kLoop, calls=%fused_computation.36 | loop fusion | flops 4206592 | bytes 6309888 | tf_op jit(solution)/shard_map/convert_element_type | solution.py:24
  75.1 42.3 %collective-permute-done.7 = f32[8,128,128]{2,1,0:T(8,128)} collective-permute-done((f32[8,128,128]{2,1,0:T(8,128)S(1)}, f32[8,128,128]{2,1,0:T(8,128)}, u32[]{:S(2)}, u32[]{:S(2)}) %collective-permute-start.7) | collective-permute-done | bytes 524320 | tf_op jit(solution)/shard_map/ppermute | solution.py:14
  118.4 1.9 %collective-permute-start.8 = (f32[8,128,128]{2,1,0:T(8,128)S(1)}, f32[8,128,128]{2,1,0:T(8,128)S(1)}, u32[]{:S(2)}, u32[]{:S(2)}) collective-permute-start(f32[8,128,128]{2,1,0:T(8,128)S(1)} %add.123), channel_id=1, source_target_pairs={{0,64},{4,68},{8,72},{12,76},{16,80},{20,84},{24,88},{28,92},{32,9... | collective-permute-start | bytes 1572872 | tf_op jit(solution)/shard_map/ppermute | solution.py:14
  120.4 2.8 %fusion.20 = bf16[128,8,8,128]{3,1,2,0:T(8,128)(2,1)S(1)} fusion(f32[1027,1024]{1,0:T(8,128)S(1)} %maximum_convert_fusion.1, f32[1024]{0:T(1024)S(1)} %bitcast.49, f32[1024]{0:T(1024)S(1)} %bitcast.50, f32[1024]{0:T(1024)S(1)} %bitcast.51, f32[1024]{0:T(1024)S(1)} %bitcast.52), kind=kLoop, calls=%fused_computation.40 | loop fusion | flops 13631488 | bytes 18890752
  123.2 1.9 %copy.20 = bf16[128,8,8,128]{3,2,1,0:T(8,128)(2,1)} copy(bf16[128,8,8,128]{3,1,2,0:T(8,128)(2,1)S(1)} %fusion.20) | data formatting | bytes 4194304
  125.6 9.4 %collective-permute-done.8 = f32[8,128,128]{2,1,0:T(8,128)S(1)} collective-permute-done((f32[8,128,128]{2,1,0:T(8,128)S(1)}, f32[8,128,128]{2,1,0:T(8,128)S(1)}, u32[]{:S(2)}, u32[]{:S(2)}) %collective-permute-start.8) | collective-permute-done | bytes 524320 | tf_op jit(solution)/shard_map/ppermute | solution.py:14
  135.9 3.6 %collective-permute-start.9 = (f32[8,128,128]{2,1,0:T(8,128)}, f32[8,128,128]{2,1,0:T(8,128)}, u32[]{:S(2)}, u32[]{:S(2)}) collective-permute-start(f32[8,128,128]{2,1,0:T(8,128)} %add.124), channel_id=1, source_target_pairs={{0,64},{4,68},{8,72},{12,76},{16,80},{20,84},{24,88},{28,92},{32,9... | collective-permute-start | bytes 1572872 | tf_op jit(solution)/shard_map/ppermute | solution.py:14
  139.5 9.3 %fusion = f32[2,8,128,512]{3,2,1,0:T(8,128)} fusion(pred[512,512]{1,0:T(8,128)(4,1)S(1)} %iota_compare_fusion, bf16[2,512,8,128]{1,3,2,0:T(8,128)(2,1)S(1)} %copy-done, bf16[2,512,8,128]{3,2,1,0:T(8,128)(2,1)} %bitcast.45, bf16[2,512,8,128]{3,2,1,0:T(8,128)(2,1)} %bitcast.44), kind=kOutput, calls=%fused_computation.1 | convolution fusion | flops 2155872256 | bytes 10747904 | tf_op jit(solution)/shard_map/nhqk,nkhd->nqhd/dot_general | solution.py:58
  148.8 3.1 %collective-permute-done.9 = f32[8,128,128]{2,1,0:T(8,128)} collective-permute-done((f32[8,128,128]{2,1,0:T(8,128)}, f32[8,128,128]{2,1,0:T(8,128)}, u32[]{:S(2)}, u32[]{:S(2)}) %collective-permute-start.9) | collective-permute-done | bytes 524320 | tf_op jit(solution)/shard_map/ppermute | solution.py:14
  153.3 5.2 %multiply_reduce_fusion = (f32[2,512]{1,0:T(2,128)S(1)}, f32[2,512,8,128]{1,3,2,0:T(8,128)}) fusion(f32[2,8,128,512]{3,2,1,0:T(8,128)} %fusion, bf16[2,512,8,128]{3,2,1,0:T(8,128)(2,1)S(1)} %bitcast.46, f32[1,8,128,128]{3,2,1,0:T(8,128)S(1)} %slice-done, f32[8,128,128]{2,1,0:T(8,128)S(1)} %add_add_fusion), kind=kOutput, calls=%fused_computation.31 | convolution fusion | flops 272104448 | bytes 11538432 | tf_op jit(solution)/shard_map/nqhd,nhde->nqhe/dot_general | solution.py:80
  158.5 5.4 %copy.17 = f32[2,512,8,128]{3,2,1,0:T(8,128)} copy(f32[2,512,8,128]{1,3,2,0:T(8,128)} %get-tuple-element.20) | data formatting | bytes 8388608 | tf_op jit(solution)/shard_map/add | solution.py:81
  163.9 10.7 %psum.7 = f32[1024]{0:T(1024)S(1)} all-reduce(f32[1024]{0:T(1024)S(1)} %bitcast.48), channel_id=1, replica_groups=mesh['ctx'=64,'head'=4] {'head'}, use_global_device_ids=true, to_apply=%region_3.4 | all-reduce | flops 1024 | bytes 8192 | tf_op jit(solution)/shard_map/psum | solution.py:82
  174.7 4.8 %fusion.7 = bf16[1024,1024]{1,0:T(8,128)(2,1)} fusion(f32[128,8,8,128]{3,2,1,0:T(8,128)} %bitcast.41, bf16[1024,1024]{1,0:T(8,128)(2,1)S(1)} %copy-done.5, f32[1024]{0:T(1024)S(1)} %copy-done.9, f32[1024]{0:T(1024)S(1)} %add_rsqrt_fusion), kind=kLoop, calls=%fused_computation.8 | loop fusion | flops 8388608 | bytes 8396800 | tf_op jit(solution)/shard_map/convert_element_type | solution.py:88
  (49 shorter events, 18.8 us)
Async XLA Ops:
  0.7 7.2 %collective-permute-start.2 = (bf16[3,1024]{1,0:T(4,128)(2,1)S(1)}, bf16[3,1024]{1,0:T(4,128)(2,1)S(1)}, u32[]{:S(2)}, u32[]{:S(2)}) collective-permute-start(bf16[3,1024]{1,0:T(4,128)(2,1)S(1)} %slice.130), channel_id=1, source_target_pairs={{0,4},{4,8},{8,12},{12,16},{16,20},{20,24},{24,28},{28,32},{32,36}... | collective-permute-start | bytes 18440 | tf_op jit(solution)/shard_map/ppermute | solution.py:14
  3.4 12.6 %collective-permute-start = (bf16[3,1024]{1,0:T(4,128)(2,1)S(1)}, bf16[3,1024]{1,0:T(4,128)(2,1)S(1)}, u32[]{:S(2)}, u32[]{:S(2)}) collective-permute-start(bf16[3,1024]{1,0:T(4,128)(2,1)S(1)} %slice.112), channel_id=1, source_target_pairs={{0,4},{4,8},{8,12},{12,16},{16,20},{20,24},{24,28},{28,32},{32,36}... | collective-permute-start | bytes 18440 | tf_op jit(solution)/shard_map/ppermute | solution.py:14
  20.1 1.6 copy-start
  20.7 18.9 %copy-start.1 = (bf16[128,8,8,128]{3,2,1,0:T(8,128)(2,1)}, bf16[128,8,8,128]{3,2,1,0:T(8,128)(2,1)S(1)}, u32[]{:S(2)}) copy-start(bf16[128,8,8,128]{3,2,1,0:T(8,128)(2,1)S(1)} %copy.19) | copy-start | bytes 6291460
  23.5 1.9 %collective-permute-start.3 = (f32[8,128,128]{2,1,0:T(8,128)S(1)}, f32[8,128,128]{2,1,0:T(8,128)S(1)}, u32[]{:S(2)}, u32[]{:S(2)}) collective-permute-start(f32[8,128,128]{2,1,0:T(8,128)S(1)} %get-tuple-element.17), channel_id=1, source_target_pairs={{0,4},{4,0},{8,12},{12,8},{16,20},{20,16},{24,28},{28,24},{32,36},... | collective-permute-start | bytes 1572872 | tf_op jit(solution)/shard_map/ppermute | solution.py:20
  25.5 14.1 %collective-permute-start.4 = (f32[8,128,128]{2,1,0:T(8,128)S(1)}, f32[8,128,128]{2,1,0:T(8,128)S(1)}, u32[]{:S(2)}, u32[]{:S(2)}) collective-permute-start(f32[8,128,128]{2,1,0:T(8,128)S(1)} %add.119), channel_id=1, source_target_pairs={{0,8},{4,12},{8,0},{12,4},{16,24},{20,28},{24,16},{28,20},{32,40},... | collective-permute-start | bytes 1572872 | tf_op jit(solution)/shard_map/ppermute | solution.py:20
  39.5 29.0 %copy-start.6 = (f32[8,128,128]{2,1,0:T(8,128)}, f32[8,128,128]{2,1,0:T(8,128)S(1)}, u32[]{:S(2)}) copy-start(f32[8,128,128]{2,1,0:T(8,128)S(1)} %collective-permute-done.4) | copy-start | bytes 1572868
  39.6 15.8 %collective-permute-start.5 = (f32[8,128,128]{2,1,0:T(8,128)S(1)}, f32[8,128,128]{2,1,0:T(8,128)S(1)}, u32[]{:S(2)}, u32[]{:S(2)}) collective-permute-start(f32[8,128,128]{2,1,0:T(8,128)S(1)} %add.120), channel_id=1, source_target_pairs={{0,16},{4,20},{8,24},{12,28},{16,0},{20,4},{24,8},{28,12},{32,48},... | collective-permute-start | bytes 1572872 | tf_op jit(solution)/shard_map/ppermute | solution.py:20
  55.4 17.2 %copy-start.7 = (f32[8,128,128]{2,1,0:T(8,128)}, f32[8,128,128]{2,1,0:T(8,128)S(1)}, u32[]{:S(2)}) copy-start(f32[8,128,128]{2,1,0:T(8,128)S(1)} %collective-permute-done.5) | copy-start | bytes 1572868
  55.5 13.0 %collective-permute-start.6 = (f32[8,128,128]{2,1,0:T(8,128)S(1)}, f32[8,128,128]{2,1,0:T(8,128)S(1)}, u32[]{:S(2)}, u32[]{:S(2)}) collective-permute-start(f32[8,128,128]{2,1,0:T(8,128)S(1)} %add.121), channel_id=1, source_target_pairs={{0,32},{4,36},{8,40},{12,44},{16,48},{20,52},{24,56},{28,60},{32,0... | collective-permute-start | bytes 1572872 | tf_op jit(solution)/shard_map/ppermute | solution.py:20
  56.4 16.5 %collective-permute-start.1 = (bf16[3,1024]{1,0:T(4,128)(2,1)S(1)}, bf16[3,1024]{1,0:T(4,128)(2,1)S(1)}, u32[]{:S(2)}, u32[]{:S(2)}) collective-permute-start(bf16[3,1024]{1,0:T(4,128)(2,1)S(1)} %slice.121), channel_id=1, source_target_pairs={{0,4},{4,8},{8,12},{12,16},{16,20},{20,24},{24,28},{28,32},{32,36}... | collective-permute-start | bytes 18440 | tf_op jit(solution)/shard_map/ppermute | solution.py:14
  68.5 4.3 %copy-start.8 = (f32[8,128,128]{2,1,0:T(8,128)}, f32[8,128,128]{2,1,0:T(8,128)S(1)}, u32[]{:S(2)}) copy-start(f32[8,128,128]{2,1,0:T(8,128)S(1)} %collective-permute-done.6) | copy-start | bytes 1572868
  68.5 48.8 %collective-permute-start.7 = (f32[8,128,128]{2,1,0:T(8,128)S(1)}, f32[8,128,128]{2,1,0:T(8,128)}, u32[]{:S(2)}, u32[]{:S(2)}) collective-permute-start(f32[8,128,128]{2,1,0:T(8,128)S(1)} %add.122), channel_id=1, source_target_pairs={{0,64},{4,68},{8,72},{12,76},{16,80},{20,84},{24,88},{28,92},{32,9... | collective-permute-start | bytes 1572872 | tf_op jit(solution)/shard_map/ppermute | solution.py:14
  118.4 16.6 %collective-permute-start.8 = (f32[8,128,128]{2,1,0:T(8,128)S(1)}, f32[8,128,128]{2,1,0:T(8,128)S(1)}, u32[]{:S(2)}, u32[]{:S(2)}) collective-permute-start(f32[8,128,128]{2,1,0:T(8,128)S(1)} %add.123), channel_id=1, source_target_pairs={{0,64},{4,68},{8,72},{12,76},{16,80},{20,84},{24,88},{28,92},{32,9... | collective-permute-start | bytes 1572872 | tf_op jit(solution)/shard_map/ppermute | solution.py:14
  123.1 2.0 %copy-start.3 = (f32[2,8,128,128]{3,2,1,0:T(8,128)S(1)}, f32[2,8,128,128]{3,2,1,0:T(8,128)}, u32[]{:S(2)}) copy-start(f32[2,8,128,128]{3,2,1,0:T(8,128)} %get-tuple-element.18) | copy-start | bytes 3145732
  125.6 10.3 %copy-start.4 = (f32[2,8,128,128]{3,2,1,0:T(8,128)}, f32[2,8,128,128]{3,2,1,0:T(8,128)S(1)}, u32[]{:S(2)}) copy-start(f32[2,8,128,128]{3,2,1,0:T(8,128)S(1)} %fusion.32) | copy-start | bytes 3145732
  135.9 16.0 %collective-permute-start.9 = (f32[8,128,128]{2,1,0:T(8,128)}, f32[8,128,128]{2,1,0:T(8,128)}, u32[]{:S(2)}, u32[]{:S(2)}) collective-permute-start(f32[8,128,128]{2,1,0:T(8,128)} %add.124), channel_id=1, source_target_pairs={{0,64},{4,68},{8,72},{12,76},{16,80},{20,84},{24,88},{28,92},{32,9... | collective-permute-start | bytes 1572872 | tf_op jit(solution)/shard_map/ppermute | solution.py:14
  139.5 13.8 %slice-start = ((f32[2,8,128,128]{3,2,1,0:T(8,128)}), f32[1,8,128,128]{3,2,1,0:T(8,128)S(1)}, s32[]{:S(2)}) async-start(f32[2,8,128,128]{3,2,1,0:T(8,128)} %copy-done.4), calls=%async_computation | async-start | bytes 1048576 | tf_op jit(solution)/shard_map/slice | solution.py:65
  148.8 4.5 %copy-start.2 = (bf16[128,8,8,128]{3,2,1,0:T(8,128)(2,1)S(1)}, bf16[128,8,8,128]{3,2,1,0:T(8,128)(2,1)}, u32[]{:S(2)}) copy-start(bf16[128,8,8,128]{3,2,1,0:T(8,128)(2,1)} %copy.20) | copy-start | bytes 6291460
  158.5 16.2 %copy-start.5 = (bf16[1024,1024]{1,0:T(8,128)(2,1)S(1)}, bf16[1024,1024]{1,0:T(8,128)(2,1)}, u32[]{:S(2)}) copy-start(bf16[1024,1024]{1,0:T(8,128)(2,1)} %param.9) | copy-start | bytes 6291460
  158.5 16.2 %copy-start.9 = (f32[1024]{0:T(1024)S(1)}, f32[1024]{0:T(1024)}, u32[]{:S(2)}) copy-start(f32[1024]{0:T(1024)} %param.11) | copy-start | bytes 12292
where the time goes:
time: 180 us; the launch traced here: 179 us
  waiting for transfers between devices  91 us (51%)
  other arithmetic  22.9 us (13%)
  starting transfers between devices  22.7 us (13%)
  matrix products  16.3 us (9%)
  local copies, waits for them, and re-layouts  15.4 us (9%)
  blocking collectives  10.7 us (6%)
    ppermute x6, waiting for transfers between devices, from_behind(): return lax.ppermute(array, axis, pairs)  54.7 us
    ppermute x4, waiting for transfers between devices, swapped(): return lax.ppermute(value, axis, pairs)  36.3 us
    ppermute x6, starting transfers between devices, from_behind(): return lax.ppermute(array, axis, pairs)  16.9 us
    psum x1, blocking collectives, body(): square = lax.psum(jnp.sum(mixed * mixed, axis=1), 'head')  10.7 us
    dot_general x1, matrix products, body(): jnp.einsum('nhqk,nkhd->nqhd', weights, value_blk, preferred_element_type=...  9.35 us
    unnamed x3, other arithmetic  7.37 us
    convert_element_type x3, other arithmetic, convolve(): jnp.concatenate([tail_rows, raw_rows], axis=0).astype(jnp.float32)  6.59 us
    ppermute x4, starting transfers between devices, swapped(): return lax.ppermute(value, axis, pairs)  5.81 us
  transfers between devices with their start and end apart: 10, of which 7 were waited for; matrix products, arithmetic and copies ran while one was open for 15% of the time, Pallas kernels for 0%

commit v1 on v0

v1 whole, which is shorter than its diff:
```python
import functools

import jax
import jax.numpy as jnp
from jax import lax
from jax.experimental import pallas as pl
from jax.experimental.pallas import tpu as pltpu
from jax.sharding import PartitionSpec as P

DH = 128
KW = 4
CHUNK = 256
STRIP = 64
TILE = 16
SLAB = 8
PAIR = 2
MESH = pl.DeviceIdType.MESH


def conv_rows(extended, taps):
    behind = pltpu.roll(extended, 1, 0)
    near = taps[3] * extended + taps[2] * behind
    far = taps[1] * extended + taps[0] * behind
    return (near + pltpu.roll(far, 2, 0))[8:]


def kernel(
    sizes,
    q_hbm,
    k_hbm,
    v_hbm,
    g_hbm,
    taps_ref,
    gain_ref,
    out_hbm,
    raw,
    cooked,
    halo,
    mixed,
    gates,
    part_state,
    send_slices,
    recv_slices,
    before,
    send_total,
    recv_total,
    send_prefix,
    prefix,
    send_square,
    recv_square,
    out_buf,
    load_sem,
    halo_send_sem,
    halo_recv_sem,
    slice_send_sem,
    slice_recv_sem,
    total_send_sem,
    total_recv_sem,
    prefix_send_sem,
    prefix_recv_sem,
    square_send_sem,
    square_recv_sem,
    store_sem,
):
    heads, tokens, slabs, ranks = sizes
    channels = heads * DH
    chunks = tokens // CHUNK
    groups = heads // PAIR
    ctx = lax.axis_index("ctx")
    rank = lax.axis_index("head")
    slab = ctx // SLAB
    place = lax.rem(ctx, SLAB)
    ctx_count = slabs * SLAB

    sources = (k_hbm, v_hbm, q_hbm, g_hbm)

    def load(array, head):
        return pltpu.make_async_copy(
            sources[array].at[:, pl.ds(pl.multiple_of(head * DH, DH), DH)],
            raw.at[array, head],
            load_sem.at[array, head],
        )

    barrier = pltpu.get_barrier_semaphore()

    def greet(target_ctx, target_rank):
        pl.semaphore_signal(
            barrier, inc=1, device_id=(target_ctx, target_rank), device_id_type=MESH
        )

    for head in range(heads):
        load(0, head).start()
        load(1, head).start()

    for step in range(1, SLAB):
        greet(slab * SLAB + lax.rem(place + step, SLAB), rank)
    for step in range(1, slabs):
        greet(lax.rem(slab + step, slabs) * SLAB + place, rank)
    for step in range(1, ranks):
        greet(ctx, lax.rem(rank + step, ranks))

    greet(lax.rem(ctx + 1, ctx_count), rank)
    greet(lax.rem(ctx + ctx_count - 1, ctx_count), rank)

    for head in range(heads):
        load(2, head).start()
    for head in range(heads):
        load(3, head).start()

    pl.semaphore_wait(barrier, SLAB - 1 + slabs - 1 + ranks - 1 + 2)

    def halo_copy(array):
        return pltpu.make_async_remote_copy(
            src_ref=sources[array].at[pl.ds(tokens - TILE, TILE), :],
            dst_ref=halo.at[array],
            send_sem=halo_send_sem.at[array],
            recv_sem=halo_recv_sem.at[array],
            device_id=(ctx + 1, rank),
            device_id_type=MESH,
        )

    @pl.when(ctx < ctx_count - 1)
    def _():
        for array in range(3):
            halo_copy(array).start()

    @pl.when(ctx == 0)
    def _():
        halo[...] = jnp.zeros_like(halo)

    def halo_wait(array):
        @pl.when(ctx > 0)
        def _():
            halo_copy(array).wait_recv()

    def lanes(head):
        return pl.ds(pl.multiple_of(head * DH, DH), DH)

    def taps_of(kind, head, factor):
        return [taps_ref[kind, j : j + 1, lanes(head)] * factor for j in range(KW)]

    def extended_rows(array, head, row):
        if row == 0:
            ahead = halo[array, :, lanes(head)]
            own = raw[array, head, 0:STRIP, :]
            return jnp.concatenate(
                [ahead.astype(jnp.float32)[8:], own.astype(jnp.float32)], axis=0
            )
        return raw[array, head, row - TILE : row + STRIP, :].astype(jnp.float32)[8:]

    def keys_values(head, chunk):
        key_taps = taps_of(1, head, 0.5)
        value_taps = taps_of(2, head, 1.0)
        first = chunk * CHUNK
        for row in range(first, first + CHUNK, STRIP):
            half = conv_rows(extended_rows(0, head, row), key_taps)
            cooked[0, head, row : row + STRIP, :] = (half + half * jnp.tanh(half)).astype(
                jnp.bfloat16
            )
            cooked[1, head, row : row + STRIP, :] = conv_rows(
                extended_rows(1, head, row), value_taps
            ).astype(jnp.bfloat16)
        part_state[head, chunk] = lax.dot_general(
            cooked[0, head, first : first + CHUNK, :],
            cooked[1, head, first : first + CHUNK, :],
            (((0,), (0,)), ((), ())),
            preferred_element_type=jnp.float32,
        )

    def finish_state(head, group, member):
        running = part_state[head, 0]
        for chunk in range(1, chunks):
            own = part_state[head, chunk]
            part_state[head, chunk] = running
            running = running + own
        part_state[head, 0] = jnp.zeros((DH, DH), jnp.float32)
        rounded = running.astype(jnp.bfloat16)
        for piece in range(SLAB):
            send_slices[group, piece, member] = rounded[piece * TILE : (piece + 1) * TILE]

    def peer(step):
        return lax.rem(place + step, SLAB)

    def slice_copy(group, step):
        return pltpu.make_async_remote_copy(
            src_ref=send_slices.at[group, peer(step)],
            dst_ref=recv_slices.at[group, step - 1],
            send_sem=slice_send_sem.at[group],
            recv_sem=slice_recv_sem.at[group],
            device_id=(slab * SLAB + peer(step), rank),
            device_id_type=MESH,
        )

    def total_copy(group, other):
        return pltpu.make_async_remote_copy(
            src_ref=send_total.at[group],
            dst_ref=recv_total.at[group, slab],
            send_sem=total_send_sem.at[group, other],
            recv_sem=total_recv_sem.at[group, slab],
            device_id=(other * SLAB + place, rank),
            device_id_type=MESH,
        )

    def total_arrival(group, other):
        return pltpu.make_async_remote_copy(
            src_ref=send_total.at[group],
            dst_ref=recv_total.at[group, other],
            send_sem=total_send_sem.at[group, other],
            recv_sem=total_recv_sem.at[group, other],
            device_id=(other * SLAB + place, rank),
            device_id_type=MESH,
        )

    def prefix_copy(group, step):
        return pltpu.make_async_remote_copy(
            src_ref=send_prefix.at[group, peer(step)],
            dst_ref=prefix.at[group, place],
            send_sem=prefix_send_sem.at[group],
            recv_sem=prefix_recv_sem.at[group],
            device_id=(slab * SLAB + peer(step), rank),
            device_id_type=MESH,
        )

    def whole(ref, sem):
        return pltpu.make_async_copy(ref, ref, sem)

    def send_states(group):
        for step in range(1, SLAB):
            slice_copy(group, step).start()

    def sum_slab(group):
        whole(recv_slices.at[group], slice_recv_sem.at[group]).wait()
        total = send_slices[group, place].astype(jnp.float32)
        for step in range(1, SLAB):
            total = total + recv_slices[group, step - 1].astype(jnp.float32)
        send_total[group] = total.astype(jnp.bfloat16)
        for other in range(1, slabs):

            @pl.when(other > slab)
            def _():
                total_copy(group, other).start()

        running = jnp.zeros((PAIR, TILE, DH), jnp.float32)
        for index in range(SLAB):
            before[group, index] = running
            if index < SLAB - 1:
                step = lax.rem(place - index + SLAB, SLAB)
                got = recv_slices[group, jnp.maximum(step - 1, 0)].astype(jnp.float32)
                own = send_slices[group, place].astype(jnp.float32)
                running = running + jnp.where(step == 0, own, got)

    def send_prefixes(group):
        def add(other, total):
            total_arrival(group, other).wait_recv()
            return total + recv_total[group, other].astype(jnp.float32)

        earlier = lax.fori_loop(0, slab, add, jnp.zeros((PAIR, TILE, DH), jnp.float32))
        for index in range(SLAB):
            send_prefix[group, index] = (earlier + before[group, index]).astype(jnp.bfloat16)
        for step in range(1, SLAB):
            prefix_copy(group, step).start()
        prefix[group, place] = send_prefix[group, place]

    def queries(head):
        query_taps = taps_of(0, head, 0.5)
        for row in range(0, tokens, STRIP):
            half = conv_rows(extended_rows(2, head, row), query_taps)
            scaled = half * DH ** (-0.5)
            cooked[2, head, row : row + STRIP, :] = (scaled + scaled * jnp.tanh(half)).astype(
                jnp.bfloat16
            )

    def inner(head):
        token = lax.broadcasted_iota(jnp.int32, (CHUNK, CHUNK), 0)
        source = lax.broadcasted_iota(jnp.int32, (CHUNK, CHUNK), 1)
        for chunk in range(chunks):
            rows = pl.ds(chunk * CHUNK, CHUNK)
            scores = lax.dot_general(
                cooked[2, head, rows, :],
                cooked[0, head, rows, :],
                (((1,), (1,)), ((), ())),
                preferred_element_type=jnp.float32,
            )
            weights = jnp.where(token >= source, scores, 0.0).astype(jnp.bfloat16)
            mixed[head, rows, :] = jnp.dot(
                weights, cooked[1, head, rows, :], preferred_element_type=jnp.float32
            )

    def gate(head):
        gain = gain_ref[pl.ds(head, 1), :] * 0.5
        for row in range(0, tokens, STRIP):
            half = raw[3, head, row : row + STRIP, :].astype(jnp.float32) * 0.5
            gates[head, row : row + STRIP, :] = gain + gain * jnp.tanh(half)

    def loop(first, last, body):
        def step(index, _):
            body(index)
            return 0

        lax.fori_loop(first, last, step, 0)

    early = heads // 2

    def later_chunks(head):
        load(0, head).wait()
        load(1, head).wait()
        for chunk in range(1, chunks):
            keys_values(head, chunk)

    loop(0, early, later_chunks)
    halo_wait(0)
    halo_wait(1)
    for group in range(groups):
        def whole_head(head):
            @pl.when(head >= early)
            def _():
                later_chunks(head)
            keys_values(head, 0)
            finish_state(head, group, head - group * PAIR)

        loop(group * PAIR, (group + 1) * PAIR, whole_head)
        send_states(group)

    halo_wait(2)

    def query_part(head):
        load(2, head).wait()
        load(3, head).wait()
        queries(head)
        inner(head)
        gate(head)

    loop(0, 1, query_part)
    sum_slab(0)
    sum_slab(1)
    loop(1, 2, query_part)
    sum_slab(2)
    loop(2, 3, query_part)
    sum_slab(3)
    loop(3, 4, query_part)
    send_prefixes(0)
    send_prefixes(1)
    loop(4, 5, query_part)
    send_prefixes(2)
    loop(5, 6, query_part)
    send_prefixes(3)
    loop(6, 8, query_part)

    for group in range(groups):
        whole(recv_slices.at[group], prefix_recv_sem.at[group]).wait()

    eye = (
        lax.broadcasted_iota(jnp.int32, (128, 128), 0)
        == lax.broadcasted_iota(jnp.int32, (128, 128), 1)
    )

    def square_copy(chunk, step):
        return pltpu.make_async_remote_copy(
            src_ref=send_square.at[chunk],
            dst_ref=recv_square.at[chunk, step - 1],
            send_sem=square_send_sem.at[chunk],
            recv_sem=square_recv_sem.at[chunk],
            device_id=(ctx, lax.rem(rank + step, ranks)),
            device_id_type=MESH,
        )

    def outer(chunk):
        rows = pl.ds(chunk * CHUNK, CHUNK)

        def add_head(head, squares):
            carried = prefix[head // PAIR, :, lax.rem(head, PAIR)].reshape(DH, DH)
            state = (carried.astype(jnp.float32) + part_state[head, chunk]).astype(jnp.bfloat16)
            here = mixed[head, rows, :] + jnp.dot(
                cooked[2, head, rows, :], state, preferred_element_type=jnp.float32
            )
            mixed[head, rows, :] = here * gates[head, rows, :]
            return squares + here * here

        squares = lax.fori_loop(0, heads, add_head, jnp.zeros((CHUNK, DH), jnp.float32))
        column = jnp.sum(squares, axis=1, keepdims=True)
        for part in range(CHUNK // 128):
            send_square[chunk, part : part + 1, :] = jnp.sum(
                jnp.where(eye, column[part * 128 : (part + 1) * 128], 0.0), axis=0, keepdims=True
            )
        for step in range(1, ranks):
            square_copy(chunk, step).start()

    def store(chunk):
        return pltpu.make_async_copy(
            out_buf.at[pl.ds(chunk * CHUNK, CHUNK), :],
            out_hbm.at[pl.ds(chunk * CHUNK, CHUNK), :],
            store_sem.at[chunk],
        )

    def finish(chunk):
        whole(recv_square.at[chunk], square_recv_sem.at[chunk]).wait()
        square = send_square[chunk, 0 : CHUNK // 128]
        for step in range(1, ranks):
            square = square + recv_square[chunk, step - 1, 0 : CHUNK // 128]
        factor = lax.rsqrt(square / (channels * ranks) + 1e-06)
        for part in range(CHUNK // 128):
            column = jnp.sum(
                jnp.where(eye, factor[part : part + 1], 0.0), axis=1, keepdims=True
            )
            spread = jnp.broadcast_to(column, (128, DH))
            first = chunk * CHUNK + part * 128
            for head in range(heads):
                out_buf[first : first + 128, head * DH : (head + 1) * DH] = (
                    mixed[head, first : first + 128, :] * spread
                ).astype(jnp.bfloat16)
        store(chunk).start()

    for chunk in range(chunks):
        outer(chunk)
        if chunk >= 2:
            finish(chunk - 2)
    finish(chunks - 2)
    finish(chunks - 1)

    for chunk in range(chunks):
        store(chunk).wait()
        whole(recv_square.at[chunk], square_send_sem.at[chunk]).wait()
    for group in range(groups):
        whole(recv_slices.at[group], slice_send_sem.at[group]).wait()
        whole(recv_slices.at[group], prefix_send_sem.at[group]).wait()
        for other in range(1, slabs):

            @pl.when(other > slab)
            def _():
                total_copy(group, other).wait_send()

    @pl.when(ctx < ctx_count - 1)
    def _():
        for array in range(3):
            halo_copy(array).wait_send()


def body(query_raw, key_raw, value_raw, gate_raw, conv_weight, norm_gain):
    tokens, channels = query_raw.shape
    heads = channels // DH
    chunks = tokens // CHUNK
    groups = heads // PAIR
    slabs = lax.axis_size("ctx") // SLAB
    ranks = lax.axis_size("head")
    anywhere = pl.BlockSpec(memory_space=pl.ANY)
    vmem = pl.BlockSpec(memory_space=pltpu.VMEM)
    dma = pltpu.SemaphoreType.DMA
    return pl.pallas_call(
        functools.partial(kernel, (heads, tokens, slabs, ranks)),
        out_shape=jax.ShapeDtypeStruct((tokens, channels), jnp.bfloat16),
        in_specs=[anywhere] * 4 + [vmem] * 2,
        out_specs=anywhere,
        scratch_shapes=[
            pltpu.VMEM((4, heads, tokens, DH), jnp.bfloat16),
            pltpu.VMEM((3, heads, tokens, DH), jnp.bfloat16),
            pltpu.VMEM((3, TILE, channels), jnp.bfloat16),
            pltpu.VMEM((heads, tokens, DH), jnp.float32),
            pltpu.VMEM((heads, tokens, DH), jnp.float32),
            pltpu.VMEM((heads, chunks, DH, DH), jnp.float32),
            pltpu.VMEM((groups, SLAB, PAIR, TILE, DH), jnp.bfloat16),
            pltpu.VMEM((groups, SLAB - 1, PAIR, TILE, DH), jnp.bfloat16),
            pltpu.VMEM((groups, SLAB, PAIR, TILE, DH), jnp.float32),
            pltpu.VMEM((groups, PAIR, TILE, DH), jnp.bfloat16),
            pltpu.VMEM((groups, slabs, PAIR, TILE, DH), jnp.bfloat16),
            pltpu.VMEM((groups, SLAB, PAIR, TILE, DH), jnp.bfloat16),
            pltpu.VMEM((groups, SLAB, PAIR, TILE, DH), jnp.bfloat16),
            pltpu.VMEM((chunks, 8, 128), jnp.float32),
            pltpu.VMEM((chunks, ranks - 1, 8, 128), jnp.float32),
            pltpu.VMEM((tokens, channels), jnp.bfloat16),
            dma((4, heads)),
            dma((3,)),
            dma((3,)),
            dma((groups,)),
            dma((groups,)),
            dma((groups, slabs)),
            dma((groups, slabs)),
            dma((groups,)),
            dma((groups,)),
            dma((chunks,)),
            dma((chunks,)),
            dma((chunks,)),
        ],
        compiler_params=pltpu.CompilerParams(
            collective_id=0, has_side_effects=True, vmem_limit_bytes=56 * 2**20
        ),
    )(
        query_raw,
        key_raw,
        value_raw,
        gate_raw,
        conv_weight,
        norm_gain.reshape(heads, DH),
    )


def solution(mesh):
    placed = (
        P("ctx", "head"),
        P("ctx", "head"),
        P("ctx", "head"),
        P("ctx", "head"),
        P(None, None, "head"),
        P("head"),
    )
    return jax.shard_map(
        body, mesh=mesh, in_specs=placed, out_specs=P("ctx", "head"), check_vma=False
    )
```

time: 180 us -> 43.2 us (0.24)
  the two profiles are of different devices: /device:TPU:96 before, /device:TPU:192 now
where the time goes in v1:
time: 43.2 us; the launch traced here: 43 us
  Pallas kernels  40 us (93%)
  local copies, waits for them, and re-layouts  3.08 us (7%)
    pallas_call x1, Pallas kernels, body(): pl.pallas_call(functools.partial(kernel, (heads, tokens, slabs, ranks)),...  40 us
    unnamed x1, local copies, waits for them, and re-layouts  3.08 us

profile of v1, /device:TPU:192, one launch (start us, length us, event | category | flops | bytes accessed | tf_op | source)
XLA Modules:
  0.0 43.0 jit_solution(1124186999987650344)
XLA Ops:
  0.0 40.0 %shard_map.64 = bf16[1024,1024]{1,0:T(8,128)(2,1)} custom-call(bf16[1024,1024]{1,0:T(8,128)(2,1)} %q_hbm.1, bf16[1024,1024]{1,0:T(8,128)(2,1)} %k_hbm.1, bf16[1024,1024]{1,0:T(8,128)(2,1)} %v_hbm.1, bf16[1024,1024]{1,0:T(8,128)(2,1)} %g_hbm.1, f32[3,4,1024]{2,1,0:T(4,128)} %taps_ref.1, f32[8,128]{1,0:T(8,128)} %bitcast.1), custom_call_target="tpu_custom_call" | custom-call | tf_op jit(solution)/shard_map/pallas_call | solution.py:448
  40.0 3.1 %copy.8 = bf16[1024,1024]{1,0:T(8,128)(2,1)} copy(bf16[1024,1024]{1,0:T(8,128)(2,1)} %shard_map.64) | data formatting | bytes 4194304

commit v2 on v1

v2 whole, which is shorter than its diff:
```python
import functools

import jax
import jax.numpy as jnp
from jax import lax
from jax.experimental import pallas as pl
from jax.experimental.pallas import tpu as pltpu
from jax.sharding import PartitionSpec as P

DH = 128
KW = 4
CHUNK = 256
STRIP = 64
TILE = 16
SLAB = 8
GROUP = 4
SUBLANES = 8
STRIDE = CHUNK // SUBLANES
HALVES = 2
MESH = pl.DeviceIdType.MESH


def conv_rows(extended, taps):
    behind = pltpu.roll(extended, 1, 0)
    near = taps[3] * extended + taps[2] * behind
    far = taps[1] * extended + taps[0] * behind
    return (near + pltpu.roll(far, 2, 0))[8:]


def kernel(
    sizes,
    q_hbm,
    k_hbm,
    v_hbm,
    g_hbm,
    taps_hbm,
    gain_hbm,
    out_ref,
    raw,
    taps_ref,
    gain_ref,
    cooked,
    tails,
    tail_pack,
    halo,
    stride_order,
    causal,
    mixed,
    gates,
    part_state,
    states,
    squares,
    send_slices,
    recv_slices,
    before,
    send_total,
    recv_total,
    send_prefix,
    prefix,
    send_square,
    recv_square,
    load_sem,
    small_sem,
    tail_sem,
    halo_send_sem,
    halo_recv_sem,
    slice_send_sem,
    slice_recv_sem,
    total_send_sem,
    total_recv_sem,
    prefix_send_sem,
    prefix_recv_sem,
    square_send_sem,
    square_recv_sem,
    ready,
):
    heads, tokens, slabs, ranks = sizes
    channels = heads * DH
    chunks = tokens // CHUNK
    groups = heads // GROUP
    ctx = lax.axis_index("ctx")
    rank = lax.axis_index("head")
    slab = ctx // SLAB
    place = lax.rem(ctx, SLAB)
    ctx_count = slabs * SLAB

    sources = (k_hbm, v_hbm, q_hbm, g_hbm)

    def load(array, head):
        return pltpu.make_async_copy(
            sources[array].at[:, pl.ds(pl.multiple_of(head * DH, DH), DH)],
            raw.at[array, head],
            load_sem.at[array, head],
        )

    barrier = pltpu.get_barrier_semaphore()

    def greet(target_ctx, target_rank):
        pl.semaphore_signal(
            barrier, inc=1, device_id=(target_ctx, target_rank), device_id_type=MESH
        )

    def load_tail(array):
        return pltpu.make_async_copy(
            sources[array].at[pl.ds(tokens - TILE, TILE), :], tails.at[array], tail_sem.at[array]
        )

    load_taps = pltpu.make_async_copy(taps_hbm, taps_ref, small_sem.at[0])
    load_gain = pltpu.make_async_copy(gain_hbm, gain_ref, small_sem.at[1])
    load_taps.start()
    for head in range(2):
        load(0, head).start()
        load(1, head).start()
    for array in range(3):
        load_tail(array).start()
    for head in range(2, heads):
        load(0, head).start()
        load(1, head).start()

    for step in range(1, SLAB):
        greet(slab * SLAB + lax.rem(place + step, SLAB), rank)
    for step in range(1, ranks):
        greet(ctx, lax.rem(rank + step, ranks))

    @pl.when(ctx > 0)
    def _():
        greet(ctx - 1, rank)

    @pl.when(ctx < ctx_count - 1)
    def _():
        greet(ctx + 1, rank)

    for other in range(1, slabs):

        @pl.when(other > slab)
        def _():
            greet(other * SLAB + place, rank)

    load_gain.start()
    for head in range(heads):
        load(2, head).start()
        load(3, head).start()

    row = lax.broadcasted_iota(jnp.int32, (CHUNK, CHUNK), 0)
    column = lax.broadcasted_iota(jnp.int32, (CHUNK, CHUNK), 1)

    def token_of(position):
        return position % SUBLANES * STRIDE + position // SUBLANES

    stride_order[...] = jnp.where(column == token_of(row), 1.0, 0.0).astype(jnp.bfloat16)
    causal[...] = jnp.where(row >= token_of(column), 1.0, 0.0).astype(jnp.bfloat16)

    halo_copy = pltpu.make_async_remote_copy(
        src_ref=tail_pack,
        dst_ref=halo,
        send_sem=halo_send_sem,
        recv_sem=halo_recv_sem,
        device_id=(ctx + 1, rank),
        device_id_type=MESH,
    )

    def lanes(head):
        return slice(head * DH, (head + 1) * DH)

    def taps_of(kind, head, factor):
        return [taps_ref[kind, j : j + 1, lanes(head)] * factor for j in range(KW)]

    first_sublane = lax.broadcasted_iota(jnp.int32, (SUBLANES, DH), 0) == 0

    def conv_strided(rows, ahead, taps):
        edge = [
            jnp.where(
                first_sublane,
                ahead[j],
                pltpu.roll(rows[CHUNK + (j - 3) * SUBLANES :][:SUBLANES], 1, 0),
            )
            for j in range(KW - 1)
        ]
        extended = jnp.concatenate(edge + [rows], axis=0)
        terms = [
            taps[j] * extended[j * SUBLANES : j * SUBLANES + CHUNK] for j in range(KW)
        ]
        return (terms[3] + terms[2]) + (terms[1] + terms[0])

    def last_rows(rows):
        return [
            pltpu.roll(rows[CHUNK + (j - 3) * SUBLANES :][:SUBLANES], 1, 0) for j in range(KW - 1)
        ]

    def in_stride_order(array, pair, chunk):
        rows = slice(chunk * CHUNK, (chunk + 1) * CHUNK)
        both = jnp.concatenate([raw[array, 2 * pair, rows], raw[array, 2 * pair + 1, rows]], axis=1)
        return jnp.dot(stride_order[...], both, preferred_element_type=jnp.float32)

    def keys_values(pair, chunk, rows_of, ahead_of):
        for member in range(2):
            head = 2 * pair + member
            here = slice(member * DH, (member + 1) * DH)
            rows = slice(chunk * CHUNK, (chunk + 1) * CHUNK)
            half = conv_strided(rows_of[0][:, here], ahead_of(0, member), taps_of(1, head, 0.5))
            cooked[0, head, rows] = (half + half * jnp.tanh(half)).astype(jnp.bfloat16)
            cooked[1, head, rows] = conv_strided(
                rows_of[1][:, here], ahead_of(1, member), taps_of(2, head, 1.0)
            ).astype(jnp.bfloat16)

    def later_chunks(pair):
        previous = [in_stride_order(array, pair, 0) for array in range(2)]
        for chunk in range(1, chunks):
            behind = [last_rows(item) for item in previous]

            def ahead_of(array, member):
                return [item[:, member * DH : (member + 1) * DH] for item in behind[array]]

            previous = [in_stride_order(array, pair, chunk) for array in range(2)]
            keys_values(pair, chunk, previous, ahead_of)

    def first_chunk(pair):
        def ahead_of(array, member):
            head = 2 * pair + member
            rows = halo[:, lanes(head)].astype(jnp.float32)
            return [rows[array * 3 + j : array * 3 + j + 1] for j in range(KW - 1)]

        keys_values(pair, 0, [in_stride_order(array, pair, 0) for array in range(2)], ahead_of)

    def product(head, chunk):
        rows = slice(chunk * CHUNK, (chunk + 1) * CHUNK)
        part_state[head, chunk] = lax.dot_general(
            cooked[0, head, rows],
            cooked[1, head, rows],
            (((0,), (0,)), ((), ())),
            preferred_element_type=jnp.float32,
        )

    def pack_tails():
        wide = lax.broadcasted_iota(jnp.int32, (TILE, channels), 0)
        key, value, query = [
            pltpu.roll(tails[array].astype(jnp.float32), 3 * (array + 1), 0) for array in range(3)
        ]
        packed = jnp.where(wide < 3, key, jnp.where(wide < 6, value, query))
        tail_pack[...] = packed.astype(jnp.bfloat16)

    def extended_rows(array, head, row):
        if row == 0:
            ahead = halo[:, lanes(head)].astype(jnp.float32)
            own = raw[array, head, 0:STRIP, :]
            return jnp.concatenate(
                [pltpu.roll(ahead, TILE - 1, 0)[:SUBLANES], own.astype(jnp.float32)], axis=0
            )
        return raw[array, head, row - TILE : row + STRIP, :].astype(jnp.float32)[8:]

    def finish_state(head, group, member):
        running = part_state[head, 0]
        for chunk in range(1, chunks):
            own = part_state[head, chunk]
            part_state[head, chunk] = running
            running = running + own
        part_state[head, 0] = jnp.zeros((DH, DH), jnp.float32)
        rounded = running.astype(jnp.bfloat16)
        for piece in range(SLAB):
            send_slices[group, piece, member] = rounded[piece * TILE : (piece + 1) * TILE]

    def peer(step):
        return lax.rem(place + step, SLAB)

    def slice_copy(group, step):
        return pltpu.make_async_remote_copy(
            src_ref=send_slices.at[group, peer(step)],
            dst_ref=recv_slices.at[group, step - 1],
            send_sem=slice_send_sem.at[group],
            recv_sem=slice_recv_sem.at[group],
            device_id=(slab * SLAB + peer(step), rank),
            device_id_type=MESH,
        )

    def total_copy(group, other):
        return pltpu.make_async_remote_copy(
            src_ref=send_total.at[group],
            dst_ref=recv_total.at[group, slab],
            send_sem=total_send_sem.at[group, other],
            recv_sem=total_recv_sem.at[group, slab],
            device_id=(other * SLAB + place, rank),
            device_id_type=MESH,
        )

    def total_arrival(group, other):
        return pltpu.make_async_remote_copy(
            src_ref=send_total.at[group],
            dst_ref=recv_total.at[group, other],
            send_sem=total_send_sem.at[group, other],
            recv_sem=total_recv_sem.at[group, other],
            device_id=(other * SLAB + place, rank),
            device_id_type=MESH,
        )

    def prefix_copy(group, step):
        return pltpu.make_async_remote_copy(
            src_ref=send_prefix.at[group, peer(step)],
            dst_ref=prefix.at[group, place],
            send_sem=prefix_send_sem.at[group],
            recv_sem=prefix_recv_sem.at[group],
            device_id=(slab * SLAB + peer(step), rank),
            device_id_type=MESH,
        )

    def whole(ref, sem):
        return pltpu.make_async_copy(ref, ref, sem)

    def send_states(group):
        for step in range(1, SLAB):
            slice_copy(group, step).start()

    def sum_slab(group):
        whole(recv_slices.at[group], slice_recv_sem.at[group]).wait()
        total = send_slices[group, place].astype(jnp.float32)
        for step in range(1, SLAB):
            total = total + recv_slices[group, step - 1].astype(jnp.float32)
        send_total[group] = total.astype(jnp.bfloat16)
        if group == 0:

            @pl.when(slab < slabs - 1)
            def _():
                pl.semaphore_wait(ready, slabs - 1 - slab)

        for other in range(1, slabs):

            @pl.when(other > slab)
            def _():
                total_copy(group, other).start()

        running = jnp.zeros((GROUP, TILE, DH), jnp.float32)
        for index in range(SLAB):
            before[group, index] = running
            if index < SLAB - 1:
                step = lax.rem(place - index + SLAB, SLAB)
                got = recv_slices[group, jnp.maximum(step - 1, 0)].astype(jnp.float32)
                own = send_slices[group, place].astype(jnp.float32)
                running = running + jnp.where(step == 0, own, got)

    def send_prefixes(group):
        def add(other, total):
            total_arrival(group, other).wait_recv()
            return total + recv_total[group, other].astype(jnp.float32)

        earlier = lax.fori_loop(0, slab, add, jnp.zeros((GROUP, TILE, DH), jnp.float32))
        for index in range(SLAB):
            send_prefix[group, index] = (earlier + before[group, index]).astype(jnp.bfloat16)
        for step in range(1, SLAB):
            prefix_copy(group, step).start()
        prefix[group, place] = send_prefix[group, place]

    def queries(head):
        query_taps = taps_of(0, head, 0.5)
        for row in range(0, tokens, STRIP):
            half = conv_rows(extended_rows(2, head, row), query_taps)
            scaled = half * DH ** (-0.5)
            cooked[2, head, row : row + STRIP, :] = (scaled + scaled * jnp.tanh(half)).astype(
                jnp.bfloat16
            )

    def inner(head):
        for chunk in range(chunks):
            rows = slice(chunk * CHUNK, (chunk + 1) * CHUNK)
            scores = lax.dot_general(
                cooked[2, head, rows],
                cooked[0, head, rows],
                (((1,), (1,)), ((), ())),
                preferred_element_type=jnp.float32,
            )
            weights = scores.astype(jnp.bfloat16) * causal[...]
            mixed[head, rows] = jnp.dot(
                weights, cooked[1, head, rows], preferred_element_type=jnp.float32
            )

    def gate(head):
        gain = gain_ref[pl.ds(head, 1), :] * 0.5
        for row in range(0, tokens, STRIP):
            half = raw[3, head, row : row + STRIP, :].astype(jnp.float32) * 0.5
            gates[head, row : row + STRIP, :] = gain + gain * jnp.tanh(half)

    pairs = heads // 2

    def pair_loads(array, pair):
        load(array, 2 * pair).wait()
        load(array, 2 * pair + 1).wait()

    load_taps.wait()
    for pair in range(pairs // 2):
        pair_loads(0, pair)
        pair_loads(1, pair)
        later_chunks(pair)

    for array in range(3):
        load_tail(array).wait()
    pack_tails()
    pl.semaphore_wait(
        barrier,
        SLAB - 1 + ranks - 1 + slab + jnp.minimum(ctx, 1) + jnp.minimum(ctx_count - 1 - ctx, 1),
    )

    @pl.when(ctx < ctx_count - 1)
    def _():
        halo_copy.start()

    for other in range(slabs - 1):

        @pl.when(other < slab)
        def _():
            pl.semaphore_signal(
                ready, inc=1, device_id=(other * SLAB + place, rank), device_id_type=MESH
            )

    for pair in range(pairs // 2, pairs):
        pair_loads(0, pair)
        pair_loads(1, pair)
        later_chunks(pair)
    for head in range(heads):
        for chunk in range(1, chunks):
            product(head, chunk)

    @pl.when(ctx == 0)
    def _():
        halo[...] = jnp.zeros_like(halo)

    @pl.when(ctx > 0)
    def _():
        halo_copy.wait_recv()

    for group in range(groups):
        for pair in range(group * GROUP // 2, (group + 1) * GROUP // 2):
            first_chunk(pair)
        for member in range(GROUP):
            product(group * GROUP + member, 0)
            finish_state(group * GROUP + member, group, member)
        send_states(group)

    load_gain.wait()
    for head in range(heads):
        load(2, head).wait()
        load(3, head).wait()

    def query_part(first, last):
        for head in range(first, last):
            queries(head)
            inner(head)
            gate(head)

    query_part(0, heads - 2)
    for group in range(groups):
        sum_slab(group)
    query_part(heads - 2, heads)
    for group in range(groups):
        send_prefixes(group)

    eye = (
        lax.broadcasted_iota(jnp.int32, (128, 128), 0)
        == lax.broadcasted_iota(jnp.int32, (128, 128), 1)
    )
    half_tokens = tokens // HALVES

    def square_copy(half, step):
        return pltpu.make_async_remote_copy(
            src_ref=send_square.at[half],
            dst_ref=recv_square.at[half, step - 1],
            send_sem=square_send_sem.at[half],
            recv_sem=square_recv_sem.at[half],
            device_id=(ctx, lax.rem(rank + step, ranks)),
            device_id_type=MESH,
        )

    def outer(group, chunk):
        rows = slice(chunk * CHUNK, (chunk + 1) * CHUNK)
        total = None
        for head in range(group * GROUP, (group + 1) * GROUP):
            here = mixed[head, rows] + jnp.dot(
                cooked[2, head, rows], states[head, chunk], preferred_element_type=jnp.float32
            )
            mixed[head, rows] = here * gates[head, rows]
            total = here * here if total is None else total + here * here
        if group > 0:
            total = total + squares[rows]
        if group < groups - 1:
            squares[rows] = total
            return
        column = jnp.sum(total, axis=1, keepdims=True)
        for part in range(CHUNK // 128):
            index = chunk * (CHUNK // 128) + part
            half, line = index // (half_tokens // 128), index % (half_tokens // 128)
            send_square[half, line : line + 1, :] = jnp.sum(
                jnp.where(eye, column[part * 128 : (part + 1) * 128], 0.0), axis=0, keepdims=True
            )

    def finish(half):
        whole(recv_square.at[half], square_recv_sem.at[half]).wait()
        square = send_square[half]
        for step in range(1, ranks):
            square = square + recv_square[half, step - 1]
        factor = lax.rsqrt(square / (channels * ranks) + 1e-06)
        for line in range(half_tokens // 128):
            column = jnp.sum(jnp.where(eye, factor[line : line + 1], 0.0), axis=1, keepdims=True)
            spread = jnp.broadcast_to(column, (128, DH))
            first = half * half_tokens + line * 128
            for head in range(heads):
                out_ref[first : first + 128, lanes(head)] = (
                    mixed[head, first : first + 128] * spread
                ).astype(jnp.bfloat16)

    send_square[...] = jnp.zeros_like(send_square)

    for group in range(groups):
        whole(recv_slices.at[group], prefix_recv_sem.at[group]).wait()
        for member in range(GROUP):
            head = group * GROUP + member
            carried = prefix[group, :, member].reshape(DH, DH).astype(jnp.float32)
            for chunk in range(chunks):
                states[head, chunk] = (carried + part_state[head, chunk]).astype(jnp.bfloat16)
        for chunk in range(chunks):
            outer(group, chunk)
            if group == groups - 1 and (chunk + 1) * CHUNK % half_tokens == 0:
                half = (chunk + 1) * CHUNK // half_tokens - 1
                for step in range(1, ranks):
                    square_copy(half, step).start()
    for half in range(HALVES):
        finish(half)

    for half in range(HALVES):
        whole(recv_square.at[half], square_send_sem.at[half]).wait()
    for group in range(groups):
        whole(recv_slices.at[group], slice_send_sem.at[group]).wait()
        whole(recv_slices.at[group], prefix_send_sem.at[group]).wait()
        for other in range(1, slabs):

            @pl.when(other > slab)
            def _():
                total_copy(group, other).wait_send()

    @pl.when(ctx < ctx_count - 1)
    def _():
        halo_copy.wait_send()


def body(query_raw, key_raw, value_raw, gate_raw, conv_weight, norm_gain):
    tokens, channels = query_raw.shape
    heads = channels // DH
    chunks = tokens // CHUNK
    groups = heads // GROUP
    slabs = lax.axis_size("ctx") // SLAB
    ranks = lax.axis_size("head")
    dma = pltpu.SemaphoreType.DMA
    return pl.pallas_call(
        functools.partial(kernel, (heads, tokens, slabs, ranks)),
        out_shape=pltpu.VMEM((tokens, channels), jnp.bfloat16),
        in_specs=[pl.BlockSpec(memory_space=pltpu.HBM)] * 6,
        out_specs=pl.BlockSpec(memory_space=pltpu.VMEM),
        scratch_shapes=[
            pltpu.VMEM((4, heads, tokens, DH), jnp.bfloat16),
            pltpu.VMEM((3, KW, channels), jnp.float32),
            pltpu.VMEM((heads, DH), jnp.float32),
            pltpu.VMEM((3, heads, tokens, DH), jnp.bfloat16),
            pltpu.VMEM((3, TILE, channels), jnp.bfloat16),
            pltpu.VMEM((TILE, channels), jnp.bfloat16),
            pltpu.VMEM((TILE, channels), jnp.bfloat16),
            pltpu.VMEM((CHUNK, CHUNK), jnp.bfloat16),
            pltpu.VMEM((CHUNK, CHUNK), jnp.bfloat16),
            pltpu.VMEM((heads, tokens, DH), jnp.float32),
            pltpu.VMEM((heads, tokens, DH), jnp.float32),
            pltpu.VMEM((heads, chunks, DH, DH), jnp.float32),
            pltpu.VMEM((heads, chunks, DH, DH), jnp.bfloat16),
            pltpu.VMEM((tokens, DH), jnp.float32),
            pltpu.VMEM((groups, SLAB, GROUP, TILE, DH), jnp.bfloat16),
            pltpu.VMEM((groups, SLAB - 1, GROUP, TILE, DH), jnp.bfloat16),
            pltpu.VMEM((groups, SLAB, GROUP, TILE, DH), jnp.float32),
            pltpu.VMEM((groups, GROUP, TILE, DH), jnp.bfloat16),
            pltpu.VMEM((groups, slabs, GROUP, TILE, DH), jnp.bfloat16),
            pltpu.VMEM((groups, SLAB, GROUP, TILE, DH), jnp.bfloat16),
            pltpu.VMEM((groups, SLAB, GROUP, TILE, DH), jnp.bfloat16),
            pltpu.VMEM((HALVES, 8, 128), jnp.float32),
            pltpu.VMEM((HALVES, ranks - 1, 8, 128), jnp.float32),
            dma((4, heads)),
            dma((2,)),
            dma((3,)),
            dma,
            dma,
            dma((groups,)),
            dma((groups,)),
            dma((groups, slabs)),
            dma((groups, slabs)),
            dma((groups,)),
            dma((groups,)),
            dma((HALVES,)),
            dma((HALVES,)),
            pltpu.SemaphoreType.REGULAR,
        ],
        compiler_params=pltpu.CompilerParams(
            collective_id=0, has_side_effects=True, vmem_limit_bytes=48 * 2**20
        ),
    )(
        *(
            pltpu.with_memory_space_constraint(item, pltpu.HBM)
            for item in (
                query_raw,
                key_raw,
                value_raw,
                gate_raw,
                conv_weight,
                norm_gain.reshape(heads, DH),
            )
        )
    )


def solution(mesh):
    placed = (
        P("ctx", "head"),
        P("ctx", "head"),
        P("ctx", "head"),
        P("ctx", "head"),
        P(None, None, "head"),
        P("head"),
    )
    return jax.shard_map(
        body, mesh=mesh, in_specs=placed, out_specs=P("ctx", "head"), check_vma=False
    )
```

time: 43.2 us -> 31.1 us (0.72)
  Pallas kernels: 40 us -> 29.7 us
  local copies, waits for them, and re-layouts: 3.08 us -> 1.32 us
    pallas_call x1, Pallas kernels: 40 us -> 29.7 us  [body(): pl.pallas_call(functools.partial(kernel, (heads, tokens, slabs, ranks)),...]
    unnamed x1, local copies, waits for them, and re-layouts: 3.08 us -> 1.32 us
where the time goes in v2:
time: 31.1 us
  Pallas kernels  29.7 us (95%)
  local copies, waits for them, and re-layouts  1.32 us (4%)
    pallas_call x1, Pallas kernels, body(): pl.pallas_call(functools.partial(kernel, (heads, tokens, slabs, ranks)),...  29.7 us
    unnamed x1, local copies, waits for them, and re-layouts  1.32 us

profile of v2, /device:TPU:192, one launch (start us, length us, event | category | flops | bytes accessed | tf_op | source)
XLA Modules:
  0.0 31.1 jit_solution(4226358300575284916)
XLA Ops:
  0.0 29.7 %shard_map.64 = bf16[1024,1024]{1,0:T(8,128)(2,1)S(1)} custom-call(bf16[1024,1024]{1,0:T(8,128)(2,1)} %q_hbm.1, bf16[1024,1024]{1,0:T(8,128)(2,1)} %k_hbm.1, bf16[1024,1024]{1,0:T(8,128)(2,1)} %v_hbm.1, bf16[1024,1024]{1,0:T(8,128)(2,1)} %g_hbm.1, f32[3,4,1024]{2,1,0:T(4,128)} %taps_hbm.1, f32[8,128]{1,0:T(8,128)} %bitcast.1), custom_call_target="tpu_custom_call" | custom-call | tf_op jit(solution)/shard_map/pallas_call | solution.py:549
  29.7 1.3 %copy.8 = bf16[1024,1024]{1,0:T(8,128)(2,1)} copy(bf16[1024,1024]{1,0:T(8,128)(2,1)S(1)} %shard_map.64) | data formatting | bytes 4194304

commit v3 on v2

--- a/solution.py
+++ b/solution.py
@@ -12,12 +12,14 @@
 CHUNK = 256
 STRIP = 64
 TILE = 16
-SLAB = 8
+SLAB = 16
 GROUP = 4
+UNITS = GROUP * (DH // TILE) // SLAB
 SUBLANES = 8
 STRIDE = CHUNK // SUBLANES
 HALVES = 2
 MESH = pl.DeviceIdType.MESH
+FAR_FIRST = sorted(range(1, SLAB), key=lambda step: (-min(step % 8, 8 - step % 8), -step))
 
 
 def conv_rows(extended, taps):
@@ -107,15 +109,16 @@
 
     load_taps = pltpu.make_async_copy(taps_hbm, taps_ref, small_sem.at[0])
     load_gain = pltpu.make_async_copy(gain_hbm, gain_ref, small_sem.at[1])
+    def start_pair(first, pair):
+        for head in (2 * pair, 2 * pair + 1):
+            load(first, head).start()
+            load(first + 1, head).start()
+
     load_taps.start()
-    for head in range(2):
-        load(0, head).start()
-        load(1, head).start()
+    start_pair(0, 0)
+    start_pair(0, 1)
     for array in range(3):
         load_tail(array).start()
-    for head in range(2, heads):
-        load(0, head).start()
-        load(1, head).start()
 
     for step in range(1, SLAB):
         greet(slab * SLAB + lax.rem(place + step, SLAB), rank)
@@ -135,11 +138,6 @@
         @pl.when(other > slab)
         def _():
             greet(other * SLAB + place, rank)
-
-    load_gain.start()
-    for head in range(heads):
-        load(2, head).start()
-        load(3, head).start()
 
     row = lax.broadcasted_iota(jnp.int32, (CHUNK, CHUNK), 0)
     column = lax.broadcasted_iota(jnp.int32, (CHUNK, CHUNK), 1)
@@ -256,8 +254,9 @@
             running = running + own
         part_state[head, 0] = jnp.zeros((DH, DH), jnp.float32)
         rounded = running.astype(jnp.bfloat16)
-        for piece in range(SLAB):
-            send_slices[group, piece, member] = rounded[piece * TILE : (piece + 1) * TILE]
+        for piece in range(DH // TILE):
+            owner = member // UNITS * (DH // TILE) + piece
+            send_slices[group, owner, member % UNITS] = rounded[piece * TILE : (piece + 1) * TILE]
 
     def peer(step):
         return lax.rem(place + step, SLAB)
@@ -306,7 +305,7 @@
         return pltpu.make_async_copy(ref, ref, sem)
 
     def send_states(group):
-        for step in range(1, SLAB):
+        for step in FAR_FIRST:
             slice_copy(group, step).start()
 
     def sum_slab(group):
@@ -321,13 +320,14 @@
             def _():
                 pl.semaphore_wait(ready, slabs - 1 - slab)
 
-        for other in range(1, slabs):
+        for other in range(slabs - 1, 0, -1):
 
             @pl.when(other > slab)
             def _():
                 total_copy(group, other).start()
 
-        running = jnp.zeros((GROUP, TILE, DH), jnp.float32)
+    def sum_before(group):
+        running = jnp.zeros((UNITS, TILE, DH), jnp.float32)
         for index in range(SLAB):
             before[group, index] = running
             if index < SLAB - 1:
@@ -341,10 +341,10 @@
             total_arrival(group, other).wait_recv()
             return total + recv_total[group, other].astype(jnp.float32)
 
-        earlier = lax.fori_loop(0, slab, add, jnp.zeros((GROUP, TILE, DH), jnp.float32))
+        earlier = lax.fori_loop(0, slab, add, jnp.zeros((UNITS, TILE, DH), jnp.float32))
         for index in range(SLAB):
             send_prefix[group, index] = (earlier + before[group, index]).astype(jnp.bfloat16)
-        for step in range(1, SLAB):
+        for step in FAR_FIRST:
             prefix_copy(group, step).start()
         prefix[group, place] = send_prefix[group, place]
 
@@ -387,6 +387,7 @@
     for pair in range(pairs // 2):
         pair_loads(0, pair)
         pair_loads(1, pair)
+        start_pair(0, pair + 2)
         later_chunks(pair)
 
     for array in range(3):
@@ -409,9 +410,12 @@
                 ready, inc=1, device_id=(other * SLAB + place, rank), device_id_type=MESH
             )
 
+    load_gain.start()
     for pair in range(pairs // 2, pairs):
         pair_loads(0, pair)
         pair_loads(1, pair)
+        start_pair(2, 2 * pair - pairs)
+        start_pair(2, 2 * pair - pairs + 1)
         later_chunks(pair)
     for head in range(heads):
         for chunk in range(1, chunks):
@@ -447,7 +451,11 @@
     query_part(0, heads - 2)
     for group in range(groups):
         sum_slab(group)
+    for group in range(groups):
+        sum_before(group)
     query_part(heads - 2, heads)
+    states[...] = jnp.zeros_like(states)
+    send_square[...] = jnp.zeros_like(send_square)
     for group in range(groups):
         send_prefixes(group)
 
@@ -470,12 +478,16 @@
     def outer(group, chunk):
         rows = slice(chunk * CHUNK, (chunk + 1) * CHUNK)
         total = None
-        for head in range(group * GROUP, (group + 1) * GROUP):
-            here = mixed[head, rows] + jnp.dot(
-                cooked[2, head, rows], states[head, chunk], preferred_element_type=jnp.float32
-            )
-            mixed[head, rows] = here * gates[head, rows]
-            total = here * here if total is None else total + here * here
+        for pair in range(group * GROUP // 2, (group + 1) * GROUP // 2):
+            both = jnp.concatenate(
+                [cooked[2, 2 * pair, rows], cooked[2, 2 * pair + 1, rows]], axis=1
+            )
+            carried = jnp.dot(both, states[pair, chunk], preferred_element_type=jnp.float32)
+            for member in range(2):
+                head = 2 * pair + member
+                here = mixed[head, rows] + carried[:, member * DH : (member + 1) * DH]
+                mixed[head, rows] = here * gates[head, rows]
+                total = here * here if total is None else total + here * here
         if group > 0:
             total = total + squares[rows]
         if group < groups - 1:
@@ -504,15 +516,18 @@
                     mixed[head, first : first + 128] * spread
                 ).astype(jnp.bfloat16)
 
-    send_square[...] = jnp.zeros_like(send_square)
-
     for group in range(groups):
         whole(recv_slices.at[group], prefix_recv_sem.at[group]).wait()
         for member in range(GROUP):
             head = group * GROUP + member
-            carried = prefix[group, :, member].reshape(DH, DH).astype(jnp.float32)
+            first = member // UNITS * (DH // TILE)
+            carried = prefix[group, first : first + DH // TILE, member % UNITS]
+            carried = carried.reshape(DH, DH).astype(jnp.float32)
             for chunk in range(chunks):
-                states[head, chunk] = (carried + part_state[head, chunk]).astype(jnp.bfloat16)
+                block = slice(head % 2 * DH, (head % 2 + 1) * DH)
+                states[head // 2, chunk, block, block] = (
+                    carried + part_state[head, chunk]
+                ).astype(jnp.bfloat16)
         for chunk in range(chunks):
             outer(group, chunk)
             if group == groups - 1 and (chunk + 1) * CHUNK % half_tokens == 0:
@@ -564,15 +579,15 @@
             pltpu.VMEM((heads, tokens, DH), jnp.float32),
             pltpu.VMEM((heads, tokens, DH), jnp.float32),
             pltpu.VMEM((heads, chunks, DH, DH), jnp.float32),
-            pltpu.VMEM((heads, chunks, DH, DH), jnp.bfloat16),
+            pltpu.VMEM((heads // 2, chunks, 2 * DH, 2 * DH), jnp.bfloat16),
             pltpu.VMEM((tokens, DH), jnp.float32),
-            pltpu.VMEM((groups, SLAB, GROUP, TILE, DH), jnp.bfloat16),
-            pltpu.VMEM((groups, SLAB - 1, GROUP, TILE, DH), jnp.bfloat16),
-            pltpu.VMEM((groups, SLAB, GROUP, TILE, DH), jnp.float32),
-            pltpu.VMEM((groups, GROUP, TILE, DH), jnp.bfloat16),
-            pltpu.VMEM((groups, slabs, GROUP, TILE, DH), jnp.bfloat16),
-            pltpu.VMEM((groups, SLAB, GROUP, TILE, DH), jnp.bfloat16),
-            pltpu.VMEM((groups, SLAB, GROUP, TILE, DH), jnp.bfloat16),
+            pltpu.VMEM((groups, SLAB, UNITS, TILE, DH), jnp.bfloat16),
+            pltpu.VMEM((groups, SLAB - 1, UNITS, TILE, DH), jnp.bfloat16),
+            pltpu.VMEM((groups, SLAB, UNITS, TILE, DH), jnp.float32),
+            pltpu.VMEM((groups, UNITS, TILE, DH), jnp.bfloat16),
+            pltpu.VMEM((groups, slabs, UNITS, TILE, DH), jnp.bfloat16),
+            pltpu.VMEM((groups, SLAB, UNITS, TILE, DH), jnp.bfloat16),
+            pltpu.VMEM((groups, SLAB, UNITS, TILE, DH), jnp.bfloat16),
             pltpu.VMEM((HALVES, 8, 128), jnp.float32),
             pltpu.VMEM((HALVES, ranks - 1, 8, 128), jnp.float32),
             dma((4, heads)),

time: 31.1 us -> 28.3 us (0.910)
  Pallas kernels: 29.7 us -> 26.6 us
    pallas_call x1, Pallas kernels: 29.7 us -> 26.6 us  [body(): pl.pallas_call(functools.partial(kernel, (heads, tokens, slabs, ranks)),...]
where the time goes in v3:
time: 28.3 us; the launch traced here: 28 us
  Pallas kernels  26.6 us (94%)
  local copies, waits for them, and re-layouts  1.32 us (5%)
    pallas_call x1, Pallas kernels, body(): pl.pallas_call(functools.partial(kernel, (heads, tokens, slabs, ranks)),...  26.6 us
    unnamed x1, local copies, waits for them, and re-layouts  1.32 us

profile of v3, /device:TPU:192, one launch (start us, length us, event | category | flops | bytes accessed | tf_op | source)
XLA Modules:
  0.0 28.0 jit_solution(3192580902137206569)
XLA Ops:
  0.0 26.6 %shard_map.64 = bf16[1024,1024]{1,0:T(8,128)(2,1)S(1)} custom-call(bf16[1024,1024]{1,0:T(8,128)(2,1)} %q_hbm.1, bf16[1024,1024]{1,0:T(8,128)(2,1)} %k_hbm.1, bf16[1024,1024]{1,0:T(8,128)(2,1)} %v_hbm.1, bf16[1024,1024]{1,0:T(8,128)(2,1)} %g_hbm.1, f32[3,4,1024]{2,1,0:T(4,128)} %taps_hbm.1, f32[8,128]{1,0:T(8,128)} %bitcast.1), custom_call_target="tpu_custom_call" | custom-call | tf_op jit(solution)/shard_map/pallas_call | solution.py:564
  26.6 1.3 %copy.8 = bf16[1024,1024]{1,0:T(8,128)(2,1)} copy(bf16[1024,1024]{1,0:T(8,128)(2,1)S(1)} %shard_map.64) | data formatting | bytes 4194304

commit v4 on v3

--- a/solution.py
+++ b/solution.py
@@ -17,6 +17,7 @@
 UNITS = GROUP * (DH // TILE) // SLAB
 SUBLANES = 8
 STRIDE = CHUNK // SUBLANES
+RIM = 32
 HALVES = 2
 MESH = pl.DeviceIdType.MESH
 FAR_FIRST = sorted(range(1, SLAB), key=lambda step: (-min(step % 8, 8 - step % 8), -step))
@@ -45,6 +46,8 @@
     tails,
     tail_pack,
     halo,
+    rim,
+    later_state,
     stride_order,
     causal,
     mixed,
@@ -165,60 +168,75 @@
 
     first_sublane = lax.broadcasted_iota(jnp.int32, (SUBLANES, DH), 0) == 0
 
-    def conv_strided(rows, ahead, taps):
-        edge = [
-            jnp.where(
-                first_sublane,
-                ahead[j],
-                pltpu.roll(rows[CHUNK + (j - 3) * SUBLANES :][:SUBLANES], 1, 0),
-            )
-            for j in range(KW - 1)
-        ]
-        extended = jnp.concatenate(edge + [rows], axis=0)
-        terms = [
-            taps[j] * extended[j * SUBLANES : j * SUBLANES + CHUNK] for j in range(KW)
-        ]
-        return (terms[3] + terms[2]) + (terms[1] + terms[0])
-
     def last_rows(rows):
         return [
             pltpu.roll(rows[CHUNK + (j - 3) * SUBLANES :][:SUBLANES], 1, 0) for j in range(KW - 1)
         ]
 
+    def conv_strided(extended, taps):
+        count = extended.shape[0] - (KW - 1) * SUBLANES
+        terms = [taps[j] * extended[j * SUBLANES : j * SUBLANES + count] for j in range(KW)]
+        return (terms[3] + terms[2]) + (terms[1] + terms[0])
+
+    def cook(array, head, rows, extended):
+        if array == 0:
+            half = conv_strided(extended, taps_of(1, head, 0.5))
+            cooked[0, head, rows] = (half + half * jnp.tanh(half)).astype(jnp.bfloat16)
+        else:
+            cooked[1, head, rows] = conv_strided(extended, taps_of(2, head, 1.0)).astype(
+                jnp.bfloat16
+            )
+
     def in_stride_order(array, pair, chunk):
         rows = slice(chunk * CHUNK, (chunk + 1) * CHUNK)
         both = jnp.concatenate([raw[array, 2 * pair, rows], raw[array, 2 * pair + 1, rows]], axis=1)
         return jnp.dot(stride_order[...], both, preferred_element_type=jnp.float32)
 
-    def keys_values(pair, chunk, rows_of, ahead_of):
-        for member in range(2):
-            head = 2 * pair + member
-            here = slice(member * DH, (member + 1) * DH)
-            rows = slice(chunk * CHUNK, (chunk + 1) * CHUNK)
-            half = conv_strided(rows_of[0][:, here], ahead_of(0, member), taps_of(1, head, 0.5))
-            cooked[0, head, rows] = (half + half * jnp.tanh(half)).astype(jnp.bfloat16)
-            cooked[1, head, rows] = conv_strided(
-                rows_of[1][:, here], ahead_of(1, member), taps_of(2, head, 1.0)
-            ).astype(jnp.bfloat16)
-
-    def later_chunks(pair):
-        previous = [in_stride_order(array, pair, 0) for array in range(2)]
-        for chunk in range(1, chunks):
-            behind = [last_rows(item) for item in previous]
-
-            def ahead_of(array, member):
-                return [item[:, member * DH : (member + 1) * DH] for item in behind[array]]
-
-            previous = [in_stride_order(array, pair, chunk) for array in range(2)]
-            keys_values(pair, chunk, previous, ahead_of)
-
-    def first_chunk(pair):
-        def ahead_of(array, member):
-            head = 2 * pair + member
-            rows = halo[:, lanes(head)].astype(jnp.float32)
-            return [rows[array * 3 + j : array * 3 + j + 1] for j in range(KW - 1)]
-
-        keys_values(pair, 0, [in_stride_order(array, pair, 0) for array in range(2)], ahead_of)
+    def keys_values(pair):
+        behind = None
+        for chunk in range(chunks):
+            rows_of = [in_stride_order(array, pair, chunk) for array in range(2)]
+            last = [last_rows(item) for item in rows_of]
+            for member in range(2):
+                head = 2 * pair + member
+                here = slice(member * DH, (member + 1) * DH)
+                for array in range(2):
+                    rows = rows_of[array][:, here]
+                    edge = [item[:, here] for item in last[array]]
+                    if chunk == 0:
+                        rim[array, head] = jnp.concatenate(edge + [rows[:RIM]], axis=0)
+                        cook(
+                            array,
+                            head,
+                            slice(RIM, CHUNK),
+                            rows[RIM - (KW - 1) * SUBLANES :],
+                        )
+                    else:
+                        edge = [
+                            jnp.where(first_sublane, before_it[:, here], after_it)
+                            for before_it, after_it in zip(behind[array], edge)
+                        ]
+                        cook(
+                            array,
+                            head,
+                            slice(chunk * CHUNK, (chunk + 1) * CHUNK),
+                            jnp.concatenate(edge + [rows], axis=0),
+                        )
+            behind = last
+
+    def finish_rim(head):
+        arrived = halo[:, lanes(head)].astype(jnp.float32)
+        for array in range(2):
+            edge = [
+                jnp.where(
+                    first_sublane,
+                    arrived[array * 3 + j : array * 3 + j + 1],
+                    rim[array, head, j * SUBLANES : (j + 1) * SUBLANES],
+                )
+                for j in range(KW - 1)
+            ]
+            rows = rim[array, head, (KW - 1) * SUBLANES :]
+            cook(array, head, slice(0, RIM), jnp.concatenate(edge + [rows], axis=0))
 
     def product(head, chunk):
         rows = slice(chunk * CHUNK, (chunk + 1) * CHUNK)
@@ -246,17 +264,25 @@
             )
         return raw[array, head, row - TILE : row + STRIP, :].astype(jnp.float32)[8:]
 
+    def sum_later(head):
+        total = part_state[head, 1]
+        for chunk in range(2, chunks):
+            total = total + part_state[head, chunk]
+        later_state[head] = total
+
     def finish_state(head, group, member):
+        rounded = (part_state[head, 0] + later_state[head]).astype(jnp.bfloat16)
+        for piece in range(DH // TILE):
+            owner = member // UNITS * (DH // TILE) + piece
+            send_slices[group, owner, member % UNITS] = rounded[piece * TILE : (piece + 1) * TILE]
+
+    def chunk_prefixes(head):
         running = part_state[head, 0]
         for chunk in range(1, chunks):
             own = part_state[head, chunk]
             part_state[head, chunk] = running
             running = running + own
         part_state[head, 0] = jnp.zeros((DH, DH), jnp.float32)
-        rounded = running.astype(jnp.bfloat16)
-        for piece in range(DH // TILE):
-            owner = member // UNITS * (DH // TILE) + piece
-            send_slices[group, owner, member % UNITS] = rounded[piece * TILE : (piece + 1) * TILE]
 
     def peer(step):
         return lax.rem(place + step, SLAB)
@@ -388,7 +414,7 @@
         pair_loads(0, pair)
         pair_loads(1, pair)
         start_pair(0, pair + 2)
-        later_chunks(pair)
+        keys_values(pair)
 
     for array in range(3):
         load_tail(array).wait()
@@ -416,10 +442,11 @@
         pair_loads(1, pair)
         start_pair(2, 2 * pair - pairs)
         start_pair(2, 2 * pair - pairs + 1)
-        later_chunks(pair)
+        keys_values(pair)
     for head in range(heads):
         for chunk in range(1, chunks):
             product(head, chunk)
+        sum_later(head)
 
     @pl.when(ctx == 0)
     def _():
@@ -430,14 +457,16 @@
         halo_copy.wait_recv()
 
     for group in range(groups):
-        for pair in range(group * GROUP // 2, (group + 1) * GROUP // 2):
-            first_chunk(pair)
+        for member in range(GROUP):
+            finish_rim(group * GROUP + member)
         for member in range(GROUP):
             product(group * GROUP + member, 0)
             finish_state(group * GROUP + member, group, member)
         send_states(group)
 
     load_gain.wait()
+    for head in range(heads):
+        chunk_prefixes(head)
     for head in range(heads):
         load(2, head).wait()
         load(3, head).wait()
@@ -574,6 +603,8 @@
             pltpu.VMEM((3, TILE, channels), jnp.bfloat16),
             pltpu.VMEM((TILE, channels), jnp.bfloat16),
             pltpu.VMEM((TILE, channels), jnp.bfloat16),
+            pltpu.VMEM((2, heads, (KW - 1) * SUBLANES + RIM, DH), jnp.float32),
+            pltpu.VMEM((heads, DH, DH), jnp.float32),
             pltpu.VMEM((CHUNK, CHUNK), jnp.bfloat16),
             pltpu.VMEM((CHUNK, CHUNK), jnp.bfloat16),
             pltpu.VMEM((heads, tokens, DH), jnp.float32),

time: 28.3 us -> 27.9 us (0.986)
  Pallas kernels: 26.6 us -> 26.2 us
    pallas_call x1, Pallas kernels: 26.6 us -> 26.2 us  [body(): pl.pallas_call(functools.partial(kernel, (heads, tokens, slabs, ranks)),...]
where the time goes in v4:
time: 27.9 us; the launch traced here: 27.6 us
  Pallas kernels  26.2 us (94%)
  local copies, waits for them, and re-layouts  1.32 us (5%)
    pallas_call x1, Pallas kernels, body(): pl.pallas_call(functools.partial(kernel, (heads, tokens, slabs, ranks)),...  26.2 us
    unnamed x1, local copies, waits for them, and re-layouts  1.32 us

profile of v4, /device:TPU:192, one launch (start us, length us, event | category | flops | bytes accessed | tf_op | source)
XLA Modules:
  0.0 27.6 jit_solution(7387211215503310419)
XLA Ops:
  0.0 26.2 %shard_map.64 = bf16[1024,1024]{1,0:T(8,128)(2,1)S(1)} custom-call(bf16[1024,1024]{1,0:T(8,128)(2,1)} %q_hbm.1, bf16[1024,1024]{1,0:T(8,128)(2,1)} %k_hbm.1, bf16[1024,1024]{1,0:T(8,128)(2,1)} %v_hbm.1, bf16[1024,1024]{1,0:T(8,128)(2,1)} %g_hbm.1, f32[3,4,1024]{2,1,0:T(4,128)} %taps_hbm.1, f32[8,128]{1,0:T(8,128)} %bitcast.1), custom_call_target="tpu_custom_call" | custom-call | tf_op jit(solution)/shard_map/pallas_call | solution.py:593
  26.2 1.3 %copy.8 = bf16[1024,1024]{1,0:T(8,128)(2,1)} copy(bf16[1024,1024]{1,0:T(8,128)(2,1)S(1)} %shard_map.64) | data formatting | bytes 4194304

commit v5 on v4

--- a/solution.py
+++ b/solution.py
@@ -393,9 +393,14 @@
                 preferred_element_type=jnp.float32,
             )
             weights = scores.astype(jnp.bfloat16) * causal[...]
-            mixed[head, rows] = jnp.dot(
-                weights, cooked[1, head, rows], preferred_element_type=jnp.float32
-            )
+            here = jnp.dot(weights, cooked[1, head, rows], preferred_element_type=jnp.float32)
+            if chunk > 0:
+                here = here + jnp.dot(
+                    cooked[2, head, rows],
+                    part_state[head, chunk].astype(jnp.bfloat16),
+                    preferred_element_type=jnp.float32,
+                )
+            mixed[head, rows] = here
 
     def gate(head):
         gain = gain_ref[pl.ds(head, 1), :] * 0.5
@@ -511,7 +516,7 @@
             both = jnp.concatenate(
                 [cooked[2, 2 * pair, rows], cooked[2, 2 * pair + 1, rows]], axis=1
             )
-            carried = jnp.dot(both, states[pair, chunk], preferred_element_type=jnp.float32)
+            carried = jnp.dot(both, states[pair], preferred_element_type=jnp.float32)
             for member in range(2):
                 head = 2 * pair + member
                 here = mixed[head, rows] + carried[:, member * DH : (member + 1) * DH]
@@ -551,12 +556,8 @@
             head = group * GROUP + member
             first = member // UNITS * (DH // TILE)
             carried = prefix[group, first : first + DH // TILE, member % UNITS]
-            carried = carried.reshape(DH, DH).astype(jnp.float32)
-            for chunk in range(chunks):
-                block = slice(head % 2 * DH, (head % 2 + 1) * DH)
-                states[head // 2, chunk, block, block] = (
-                    carried + part_state[head, chunk]
-                ).astype(jnp.bfloat16)
+            block = slice(head % 2 * DH, (head % 2 + 1) * DH)
+            states[head // 2, block, block] = carried.reshape(DH, DH)
         for chunk in range(chunks):
             outer(group, chunk)
             if group == groups - 1 and (chunk + 1) * CHUNK % half_tokens == 0:
@@ -610,7 +611,7 @@
             pltpu.VMEM((heads, tokens, DH), jnp.float32),
             pltpu.VMEM((heads, tokens, DH), jnp.float32),
             pltpu.VMEM((heads, chunks, DH, DH), jnp.float32),
-            pltpu.VMEM((heads // 2, chunks, 2 * DH, 2 * DH), jnp.bfloat16),
+            pltpu.VMEM((heads // 2, 2 * DH, 2 * DH), jnp.bfloat16),
             pltpu.VMEM((tokens, DH), jnp.float32),
             pltpu.VMEM((groups, SLAB, UNITS, TILE, DH), jnp.bfloat16),
             pltpu.VMEM((groups, SLAB - 1, UNITS, TILE, DH), jnp.bfloat16),

time: 27.9 us -> 27.9 us (level)
  no operation moved by 1% of the time
where the time goes in v5:
time: 27.9 us; the launch traced here: 27.5 us
  Pallas kernels  26.2 us (94%)
  local copies, waits for them, and re-layouts  1.32 us (5%)
    pallas_call x1, Pallas kernels, body(): pl.pallas_call(functools.partial(kernel, (heads, tokens, slabs, ranks)),...  26.2 us
    unnamed x1, local copies, waits for them, and re-layouts  1.32 us

profile of v5, /device:TPU:192, one launch (start us, length us, event | category | flops | bytes accessed | tf_op | source)
XLA Modules:
  0.0 27.5 jit_solution(14132253674720438984)
XLA Ops:
  0.0 26.2 %shard_map.64 = bf16[1024,1024]{1,0:T(8,128)(2,1)S(1)} custom-call(bf16[1024,1024]{1,0:T(8,128)(2,1)} %q_hbm.1, bf16[1024,1024]{1,0:T(8,128)(2,1)} %k_hbm.1, bf16[1024,1024]{1,0:T(8,128)(2,1)} %v_hbm.1, bf16[1024,1024]{1,0:T(8,128)(2,1)} %g_hbm.1, f32[3,4,1024]{2,1,0:T(4,128)} %taps_hbm.1, f32[8,128]{1,0:T(8,128)} %bitcast.1), custom_call_target="tpu_custom_call" | custom-call | tf_op jit(solution)/shard_map/pallas_call | solution.py:594
  26.2 1.3 %copy.8 = bf16[1024,1024]{1,0:T(8,128)(2,1)} copy(bf16[1024,1024]{1,0:T(8,128)(2,1)S(1)} %shard_map.64) | data formatting | bytes 4194304
